TPU v7x, 32 devices: a whole 2x2x4 slice. The times are simulated.
32 devices in a mesh: groups: 2 (over y), replica: 4 (over x, core), mp: 4 (over z).
Axes of the slice: x: 2, y: 2, z: 4, core: 2. Of those that a mesh axis runs over, the one named last changes fastest.
Arguments:
- tokens: bfloat16 [8192, 8192], P(('groups', 'replica'), 'mp'), parts along dimension 0, may hold values from -6 to 6
- token_adapter_index: int32 [8192], P(('groups', 'replica')), parts along dimension 0, may hold values from 0 to 31, as said below
- key_value_weight: bfloat16 [8192, 2048], P(None, 'mp'), may hold values from -0.0625 to 0.0625
- adapter_down_weight: bfloat16 [32, 64, 8192], P('replica', None, 'mp'), may hold values from -0.0625 to 0.0625
- adapter_up_weight: bfloat16 [32, 64, 2048], P('replica', None, 'mp'), may hold values from -0.75 to 0.75
Outputs:
- kv_out: bfloat16 [8192, 2048], P(('groups', 'replica'), 'mp'), parts along dimension 0
There are 2 independent parts, one for each index of `groups`. A program takes and returns all parts, laid end to end along the dimension named above; an argument that names none is the same for every part. Nothing has to cross between parts.
Inputs may be any that keep to these rules, and one draw needn't show every extreme that they name: `token_adapter_index`: adapter a is held by index a // 8 of replica. Among the 1024 tokens of one index of replica no adapter id appears more than 32 times, and one adapter id appears exactly 32 times in the tokens of every index of replica. Among them at most 256 have adapters held by one index of replica, and exactly 256 do for one index of replica in the tokens of every index of replica.
All inputs are finite; a program needn't handle non-finite values.
Results may differ from a plain program's by a relative error of at most 0.005.
Values may be sent and summed in bfloat16 or wider, within the bound.
A program may use at most 128 MiB of HBM per device.

v0:
```python
import jax
import jax.numpy as jnp
from jax import lax
from jax.sharding import PartitionSpec as P

MOST = 32


def shards(tokens, token_adapter_index, key_value_weight, adapter_down_weight, adapter_up_weight):
    owners = lax.axis_size("replica")
    owned_adapter_list = adapter_down_weight.shape[0]
    adapters_all = owners * owned_adapter_list
    feat_width = tokens.shape[1]
    kv_cols = key_value_weight.shape[1]
    labels = jnp.arange(adapters_all, dtype=jnp.int32)
    onehot = (token_adapter_index[:, None] == labels[None, :]).astype(jnp.int32)
    before = jnp.cumsum(onehot, axis=0) - onehot
    within = jnp.sum(before * onehot, axis=1)
    slot_index = token_adapter_index * MOST + within
    outgoing = jnp.zeros((adapters_all * MOST, feat_width), jnp.bfloat16).at[slot_index].set(tokens)
    outgoing = outgoing.reshape(owners, owned_adapter_list, MOST, feat_width)
    partial_rank = jnp.einsum(
        "najd,ard->najr",
        lax.all_to_all(outgoing, "replica", split_axis=0, concat_axis=0, tiled=True),
        adapter_down_weight,
        preferred_element_type=jnp.float32,
    )
    reduced_input = lax.psum(partial_rank, "mp").astype(jnp.bfloat16)
    delta_columns = jnp.einsum(
        "lcdq,cqx->lcdx", reduced_input, adapter_up_weight, preferred_element_type=jnp.float32
    ).astype(jnp.bfloat16)
    returned = lax.all_to_all(delta_columns, "replica", split_axis=0, concat_axis=0, tiled=True)
    returned = returned.reshape(adapters_all * MOST, kv_cols)
    delta_rows = returned[slot_index]
    base_out = jnp.dot(
        lax.all_gather(tokens, "mp", axis=1, tiled=True),
        key_value_weight,
        preferred_element_type=jnp.float32,
    )
    return (base_out + delta_rows.astype(jnp.float32)).astype(jnp.bfloat16)


def solution(mesh):
    return jax.shard_map(
        shards,
        mesh=mesh,
        in_specs=(
            P(("groups", "replica"), "mp"),
            P(("groups", "replica")),
            P(None, "mp"),
            P("replica", None, "mp"),
            P("replica", None, "mp"),
        ),
        out_specs=P(("groups", "replica"), "mp"),
        check_vma=False,
    )
```

profile of v0, /device:TPU:0, one launch (start us, length us, event | category | flops | bytes accessed | tf_op | source)
XLA Modules:
  0.0 337.8 jit_solution(13223298096728573039)
XLA Ops:
  6.5 0.0 copy-start
  6.5 0.0 copy-start.2
  6.5 0.0 all-gather.2.cloned.1.call-start
  6.5 0.7 all-gather.2.cloned.1.call-update
  7.3 0.1 copy-done.2
  7.4 9.0 %reduce-window.6 = s32[32,8,128]{2,1,0:T(8,128)S(1)} reduce-window(s32[32,8,128]{2,1,0:T(8,128)S(1)} %fusion.16, s32[]{:T(128)} %constant.3.clone.1), window={size=1x1x128 pad=0_0x0_0x127_0}, to_apply=%region_0.0 | reduce-window | flops 4161536 | bytes 262148 | tf_op jit(solution)/shard_map/reduce-window
  16.4 0.1 slice.10
  16.5 0.1 copy.16
  16.7 0.1 copy.17
  16.7 0.1 broadcast_add_fusion
  16.9 10.4 %scatter_custom_fusion = bf16[1024,2048]{1,0:T(8,128)(2,1)} fusion(s32[1024]{0:T(1024)S(1)} %get-tuple-element.6, bf16[1024,2048]{1,0:T(8,128)(2,1)} %param.5, bf16[]{:T(256)} %constant.4.clone.1), kind=kCustom, calls=%fused_computation.6 | custom fusion | bytes 4194816 | tf_op jit(solution)/shard_map/scatter | solution.py:20
  27.3 52.6 %all_to_all.10 = bf16[4,8,32,2048]{3,2,1,0:T(8,128)(2,1)S(1)} all-to-all(bf16[4,8,32,2048]{3,2,1,0:T(8,128)(2,1)} %bitcast.41), channel_id=1, replica_groups=mesh['groups'=2,'replica'=4,'mp'=4] {'replica'}, dimensions={0} | all-to-all | bytes 8388608 | tf_op jit(solution)/shard_map/all_to_all | solution.py:24
  79.9 0.0 copy-done
  79.9 0.0 copy-start.1
  79.9 1.2 fusion.6
  81.2 58.6 %all-reduce.1 = bf16[4,8,32,64]{3,2,0,1:T(8,128)(2,1)S(1)} all-reduce(f32[4,8,32,64]{3,2,0,1:T(8,128)S(1)} %fusion.6), channel_id=1, replica_groups=mesh['groups'=2,'replica'=4,'mp'=4] {'mp'}, use_global_device_ids=true, to_apply=%region_4.5 | all-reduce | flops 65536 | bytes 393216 | tf_op jit(solution)/shard_map/psum | solution.py:28
  139.8 0.0 copy-done.1
  139.8 0.4 fusion.5
  140.2 0.1 copy.19
  140.3 17.2 %all_to_all.11 = bf16[4,8,32,512]{3,2,1,0:T(8,128)(2,1)S(1)} all-to-all(bf16[4,8,32,512]{3,2,1,0:T(8,128)(2,1)S(1)} %copy.19), channel_id=1, replica_groups=mesh['groups'=2,'replica'=4,'mp'=4] {'replica'}, dimensions={0} | all-to-all | bytes 2097152 | tf_op jit(solution)/shard_map/all_to_all | solution.py:32
  157.5 5.1 %gather_fusion = bf16[1024,512]{1,0:T(8,128)(2,1)} fusion(bf16[1024,512]{1,0:T(8,128)(2,1)S(1)} %bitcast.40, s32[1024]{0:T(1024)S(1)} %get-tuple-element.5), kind=kCustom, calls=%fused_computation | custom fusion | bytes 2101248 | tf_op jit(solution)/shard_map/gather | solution.py:34
  162.6 152.6 %all-gather.2.cloned.1.call-done = bf16[1024,8192]{1,0:T(8,128)(2,1)} async-done(((bf16[1024,2048]{1,0:T(8,128)(2,1)}), bf16[1024,8192]{1,0:T(8,128)(2,1)}) %all-gather.2.cloned.1.call-update) | async-done | bytes 16777232 | tf_op jit(solution)/shard_map/all_gather | solution.py:36
  315.2 15.7 %add_convert_fusion = bf16[1024,512]{1,0:T(8,128)(2,1)} fusion(bf16[1024,512]{1,0:T(8,128)(2,1)} %gather_fusion, bf16[1024,8192]{1,0:T(8,128)(2,1)} %all-gather.2.cloned.1.call-done, bf16[8192,512]{1,0:T(8,128)(2,1)} %param.7), kind=kOutput, calls=%fused_computation.5 | convolution fusion | flops 8591507456 | bytes 27262976 | tf_op jit(solution)/shard_map/dot_general | solution.py:35
  (5 shorter events, 0.1 us)
Async XLA Ops:
  6.5 73.4 %copy-start = (bf16[8,64,2048]{2,1,0:T(8,128)(2,1)S(1)}, bf16[8,64,2048]{2,1,0:T(8,128)(2,1)}, u32[]{:S(2)}) copy-start(bf16[8,64,2048]{2,1,0:T(8,128)(2,1)} %param.8) | copy-start | bytes 6291460
  6.5 0.8 copy-start.2
  6.5 308.7 %all-gather.2.cloned.1.call-start = ((), (), s32[]{:S(2)}) async-start(), calls=%async_computation.2 | async-start | bytes 20971520 | tf_op jit(solution)/shard_map/all_gather | solution.py:36
  79.9 59.9 %copy-start.1 = (bf16[8,64,512]{2,1,0:T(8,128)(2,1)S(1)}, bf16[8,64,512]{2,1,0:T(8,128)(2,1)}, u32[]{:S(2)}) copy-start(bf16[8,64,512]{2,1,0:T(8,128)(2,1)} %param.9) | copy-start | bytes 1572868
Sparse Core Ops, SparseCore 0:
  8.9 306.2 all-gather.1
where the time goes:
time: 338 us
  waiting for transfers between devices  153 us (45%)
  blocking collectives  128 us (38%)
  matrix products  17.3 us (5%)
  local copies, waits for them, and re-layouts  16 us (5%)
  between operations  13.5 us (4%)
  other arithmetic  9.21 us (3%)
    all_gather x1, waiting for transfers between devices, shards(): lax.all_gather(tokens, 'mp', axis=1, tiled=True)  153 us
    psum x1, blocking collectives, shards(): reduced_input = lax.psum(partial_rank, 'mp').astype(jnp.bfloat16)  58.6 us
    all_to_all x1, blocking collectives, shards(): lax.all_to_all(outgoing, 'replica', split_axis=0, concat_axis=0, tiled=True)  52.6 us
    all_to_all x1, blocking collectives, shards(): lax.all_to_all(delta_columns, 'replica', split_axis=0, concat_axis=0, til...  17.2 us
    dot_general x1, matrix products, shards(): jnp.dot(lax.all_gather(tokens, 'mp', axis=1, tiled=True), key_value_weigh...  15.7 us
    scatter x1, local copies, waits for them, and re-layouts, shards(): jnp.zeros((adapters_all * MOST, feat_width), jnp.bfloat16).at[slot_index]  10.4 us
    another operation x3, other arithmetic  9.15 us
  transfers between devices with their start and end apart: 1, of which 1 were waited for; matrix products, arithmetic and copies ran while one was open for 8% of the time, Pallas kernels for 0%

commit v1 on v0

v1 whole, which is shorter than its diff:
```python
import functools

import jax
import jax.numpy as jnp
from jax import lax
from jax.experimental import pallas as pl
from jax.experimental.pallas import tpu as pltpu
from jax.sharding import PartitionSpec as P

BF16 = jnp.bfloat16
F32 = jnp.float32
MESH = pl.DeviceIdType.MESH


def kernel(
    G, R, Z, CH,
    tok_hbm, idx_ref, w_hbm, down_hbm, up_hbm, out_ref,
    tok, wbuf, dbuf, from_left, from_right, sendbuf, low, lowin, base,
    loc_sem, wz_s, wz_r, wp_s, wp_r, ws_s, ws_r,
    rl_s, rl_r, rr_s, rr_r,
    d0_s, d0_r, d1_s, d1_r, d2_s, d2_r, d3_s, d3_r,
    lo_s, lo_r,
):
    T, F = tok.shape
    N = w_hbm.shape[1]
    AR = down_hbm.shape[0]
    X = R // 2
    C = G * X
    FP = F // (G * R)
    HALF = AR // G
    M = T // CH

    g = lax.axis_index("groups")
    r = lax.axis_index("replica")
    z = lax.axis_index("mp")
    x = r // 2
    c = r % 2
    p = g * R + r
    q = g * X + x
    sib = (g, x * 2 + 1 - c, z)

    def chip(k):
        qq = lax.rem(q + k, C)
        return qq, (qq // X, (qq % X) * 2 + c, z)

    barrier = pltpu.get_barrier_semaphore()
    for k in range(1, Z):
        pl.semaphore_signal(barrier, inc=1, device_id=(g, r, lax.rem(z + k, Z)), device_id_type=MESH)
    for k in range(1, C):
        pl.semaphore_signal(barrier, inc=1, device_id=chip(k)[1], device_id_type=MESH)
    pl.semaphore_signal(barrier, inc=1, device_id=sib, device_id_type=MESH)

    own_d = pl.ds(pl.multiple_of(r * AR, AR), AR)
    cp_tok = pltpu.make_async_copy(tok_hbm, tok, loc_sem.at[0])
    cp_w = pltpu.make_async_copy(
        w_hbm.at[pl.ds(pl.multiple_of(z * F, F), F), :], wbuf.at[z], loc_sem.at[1])
    cp_d = pltpu.make_async_copy(down_hbm, dbuf.at[own_d, pl.ds(0, F)], loc_sem.at[2])
    cp_u = pltpu.make_async_copy(up_hbm, dbuf.at[own_d, pl.ds(F, N)], loc_sem.at[3])
    cp_tok.start()
    cp_d.start()
    cp_u.start()
    cp_w.start()
    pl.semaphore_wait(barrier, (Z - 1) + (C - 1) + 1)

    def remote(src, dst, s, rs, dev):
        return pltpu.make_async_remote_copy(
            src_ref=src, dst_ref=dst, send_sem=s, recv_sem=rs, device_id=dev, device_id_type=MESH)

    def wrows(gg, rr):
        return pl.ds(pl.multiple_of((gg * R + rr) * FP, FP), FP)

    def wz(to):
        return remote(
            w_hbm.at[pl.ds(pl.multiple_of(to * F + p * FP, FP), FP), :],
            wbuf.at[z, wrows(g, r), :], wz_s.at[to], wz_r.at[z], (g, r, to))

    def wz_in(b):
        ref = wbuf.at[b, wrows(g, r), :]
        return remote(ref, ref, wz_s.at[b], wz_r.at[b], (g, r, b))

    def wp(b, k):
        qq, dev = chip(k)
        ref = wbuf.at[b, wrows(g, r), :]
        return remote(ref, ref, wp_s.at[b, k], wp_r.at[b, q], dev)

    def wp_in(b, k):
        qq, dev = chip(k)
        ref = wbuf.at[b, wrows(qq // X, (qq % X) * 2 + c), :]
        return remote(ref, ref, wp_s.at[b, k], wp_r.at[b, qq], dev)

    def ws(b, k):
        qq, dev = chip(k)
        ref = wbuf.at[b, wrows(qq // X, (qq % X) * 2 + c), :]
        return remote(ref, ref, ws_s.at[b, qq], ws_r.at[b, qq], sib)

    def ws_in(b, k):
        qq, dev = chip(k)
        ref = wbuf.at[b, wrows(qq // X, (qq % X) * 2 + 1 - c), :]
        return remote(ref, ref, ws_s.at[b, qq], ws_r.at[b, qq], sib)

    def gather_w(b):
        wz_in(b).wait_recv()
        for k in range(1, C):
            wp(b, k).start()
        ws(b, 0).start()
        for k in range(1, C):
            wp_in(b, k).wait_recv()
            ws(b, k).start()
        for k in range(C):
            ws_in(b, k).wait_recv()

    for s in range(Z - 1):
        @pl.when(Z - 1 - s > z)
        def _(s=s):
            wz(Z - 1 - s).start()

        @pl.when(s < z)
        def _(s=s):
            wz(s).start()

    def drows(rr, h):
        return pl.ds(pl.multiple_of(rr * AR + h * HALF, HALF), HALF)

    def d0():
        ref = dbuf.at[own_d, :]
        return remote(ref, ref, d0_s, d0_r, sib)

    def d0_in():
        ref = dbuf.at[pl.ds(pl.multiple_of((x * 2 + 1 - c) * AR, AR), AR), :]
        return remote(ref, ref, d0_s, d0_r, sib)

    def d1(k):
        ref = dbuf.at[drows(r, g), :]
        return remote(ref, ref, d1_s.at[k], d1_r.at[x], (g, lax.rem(x + k, X) * 2 + c, z))

    def xk(k):
        return lax.rem(x + k, X)

    def d1_in(k):
        ref = dbuf.at[drows(xk(k) * 2 + c, g), :]
        return remote(ref, ref, d1_s.at[k], d1_r.at[xk(k)], (g, xk(k) * 2 + c, z))

    def d2(k, j):
        ref = dbuf.at[drows(xk(k) * 2 + c, g), :]
        return remote(ref, ref, d2_s.at[k, j], d2_r.at[xk(k), g], (lax.rem(g + j, G), r, z))

    def d2_in(k, j):
        gg = lax.rem(g + j, G)
        ref = dbuf.at[drows(xk(k) * 2 + c, gg), :]
        return remote(ref, ref, d2_s.at[k, j], d2_r.at[xk(k), gg], (gg, r, z))

    def d3(k, h):
        ref = dbuf.at[drows(xk(k) * 2 + c, h), :]
        return remote(ref, ref, d3_s.at[xk(k), h], d3_r.at[xk(k), h], sib)

    def d3_in(k, h):
        ref = dbuf.at[drows(xk(k) * 2 + 1 - c, h), :]
        return remote(ref, ref, d3_s.at[xk(k), h], d3_r.at[xk(k), h], sib)

    lane_half = lax.broadcasted_iota(jnp.int32, (CH, 128), 1) // 64

    def rows(m):
        return pl.ds(pl.multiple_of(m * CH, CH), CH)

    low[...] = jnp.zeros_like(low)

    def shrink(rr):
        src = pl.ds(pl.multiple_of(rr * AR, AR), AR)

        @pl.loop(0, M)
        def _(m):
            y = lax.dot_general(
                tok[rows(m), :], dbuf[src, pl.ds(0, F)], (((1,), (1,)), ((), ())),
                preferred_element_type=F32)
            mine = idx_ref[rows(m), :] - rr * (AR // 64) - lane_half
            part = low[rows(m), :]
            for t in range(AR // 128):
                part += jnp.where(mine == 2 * t, y[:, t * 128:(t + 1) * 128], 0.0)
            low[rows(m), :] = part

    cp_tok.wait()
    cp_d.wait()
    cp_u.wait()
    d0().start()
    shrink(r)

    def to_right(b, m):
        return remote(sendbuf.at[b, rows(m), :], from_left.at[b, rows(m), :],
                      rl_s.at[b, m], rl_r.at[b, m], (g, r, lax.rem(z + 1, Z)))

    def to_left(b, m):
        return remote(sendbuf.at[b, rows(m), :], from_right.at[b, rows(m), :],
                      rr_s.at[b, m], rr_r.at[b, m], (g, r, lax.rem(z + Z - 1, Z)))

    def chain(b, landed, make, first):
        @pl.loop(0, M)
        def _(m):
            y = jnp.dot(tok[rows(m), :], wbuf[b], preferred_element_type=F32)

            @pl.when(first)
            def _():
                sendbuf[b, rows(m), :] = y.astype(BF16)

            @pl.when(jnp.logical_not(first))
            def _():
                make(b, m).wait_recv()
                sendbuf[b, rows(m), :] = (y + landed[b, rows(m), :].astype(F32)).astype(BF16)

            make(b, m).start()

    for s in range(Z - 1):
        @pl.when(Z - 1 - s > z)
        def _(b=Z - 1 - s):
            gather_w(b)
            chain(b, from_left, to_right, z == 0)

        @pl.when(s < z)
        def _(b=s):
            gather_w(b)
            chain(b, from_right, to_left, z == Z - 1)

        if s == 0:
            for k in range(1, X):
                d1(k).start()

    for k in range(1, X):
        d1_in(k).wait_recv()
        for j in range(1, G):
            d2(k, j).start()
        d3(k, g).start()
    d0_in().wait_recv()
    shrink(x * 2 + 1 - c)
    for k in range(1, X):
        for j in range(1, G):
            d2_in(k, j).wait_recv()
            d3(k, lax.rem(g + j, G)).start()
        shrink(xk(k) * 2 + c)
    for k in range(1, X):
        for h in range(G):
            d3_in(k, h).wait_recv()
        shrink(xk(k) * 2 + 1 - c)

    H = T // 2
    left_lanes = lax.broadcasted_iota(jnp.int32, (H, 128), 1) < 64
    both = low[...]
    both = both + pltpu.roll(both, 64, 1)
    packed = jnp.where(left_lanes, both[:H], both[H:])
    lowin[z] = packed.astype(BF16)

    def lo(k):
        return remote(lowin.at[z], lowin.at[z], lo_s.at[k], lo_r.at[z], (g, r, lax.rem(z + k, Z)))

    def lo_in(k):
        zz = lax.rem(z + k, Z)
        return remote(lowin.at[zz], lowin.at[zz], lo_s.at[k], lo_r.at[zz], (g, r, zz))

    for k in range(1, Z):
        lo(k).start()

    cp_w.wait()

    @pl.loop(0, M)
    def _(m):
        base[rows(m), :] = jnp.dot(tok[rows(m), :], wbuf[z], preferred_element_type=F32)

    total = packed
    for k in range(1, Z):
        lo_in(k).wait_recv()
        total = total + lowin[lax.rem(z + k, Z)].astype(F32)
    total = total.astype(BF16).astype(F32)
    other = pltpu.roll(total, 64, 1)
    low[pl.ds(0, H), :] = jnp.where(left_lanes, total, other)
    low[pl.ds(H, H), :] = jnp.where(left_lanes, other, total)

    @pl.loop(0, M)
    def _(m):
        ss = low[rows(m), :]
        who = idx_ref[rows(m), :] - lane_half

        def add(rr, acc):
            lhs = jnp.concatenate(
                [jnp.where(who == rr * (AR // 64) + 2 * t, ss, 0.0).astype(BF16) for t in range(AR // 128)],
                axis=1)
            return acc + jnp.dot(
                lhs, dbuf[pl.ds(pl.multiple_of(rr * AR, AR), AR), pl.ds(F, N)],
                preferred_element_type=F32)

        delta = lax.fori_loop(0, R, add, jnp.zeros((CH, N), F32))
        base[rows(m), :] = base[rows(m), :] + delta.astype(BF16).astype(F32)

    @pl.when(z > 0)
    def _():
        @pl.loop(0, M)
        def _(m):
            to_right(z, m).wait_recv()
            base[rows(m), :] = base[rows(m), :] + from_left[z, rows(m), :].astype(F32)

    @pl.when(z < Z - 1)
    def _():
        @pl.loop(0, M)
        def _(m):
            to_left(z, m).wait_recv()
            base[rows(m), :] = base[rows(m), :] + from_right[z, rows(m), :].astype(F32)

    out_ref[...] = base[...].astype(BF16)

    for b in range(Z):
        @pl.when(b != z)
        def _(b=b):
            wz(b).wait_send()
            for k in range(1, C):
                wp(b, k).wait_send()
            for k in range(C):
                ws(b, k).wait_send()

        @pl.when(b > z)
        def _(b=b):
            @pl.loop(0, M)
            def _(m):
                to_right(b, m).wait_send()

        @pl.when(b < z)
        def _(b=b):
            @pl.loop(0, M)
            def _(m):
                to_left(b, m).wait_send()
    d0().wait_send()
    for k in range(1, X):
        d1(k).wait_send()
        for j in range(1, G):
            d2(k, j).wait_send()
        for h in range(G):
            d3(k, h).wait_send()
    for k in range(1, Z):
        lo(k).wait_send()


def shards(G, R, Z, tokens, token_adapter_index, key_value_weight, adapter_down_weight, adapter_up_weight):
    T, F = tokens.shape
    N = key_value_weight.shape[1]
    A, K, _ = adapter_down_weight.shape
    AR = A * K
    CH = min(256, T)
    M = T // CH
    X = R // 2
    C = G * X
    idx = jnp.broadcast_to(token_adapter_index[:, None], (T, 128))
    dma = pltpu.SemaphoreType.DMA
    any_spec = pl.BlockSpec(memory_space=pl.ANY)
    vmem_spec = pl.BlockSpec(memory_space=pltpu.VMEM)
    return pl.pallas_call(
        functools.partial(kernel, G, R, Z, CH),
        out_shape=jax.ShapeDtypeStruct((T, N), BF16),
        in_specs=[any_spec, vmem_spec, any_spec, any_spec, any_spec],
        out_specs=vmem_spec,
        scratch_shapes=[
            pltpu.VMEM((T, F), BF16),
            pltpu.VMEM((Z, F, N), BF16),
            pltpu.VMEM((R * AR, F + N), BF16),
            pltpu.VMEM((Z, T, N), BF16),
            pltpu.VMEM((Z, T, N), BF16),
            pltpu.VMEM((Z, T, N), BF16),
            pltpu.VMEM((T, 128), F32),
            pltpu.VMEM((Z, T // 2, 128), BF16),
            pltpu.VMEM((T, N), F32),
            dma((4,)), dma((Z,)), dma((Z,)), dma((Z, C)), dma((Z, C)), dma((Z, C)), dma((Z, C)),
            dma((Z, M)), dma((Z, M)), dma((Z, M)), dma((Z, M)),
            dma, dma, dma((X,)), dma((X,)), dma((X, G)), dma((X, G)), dma((X, G)), dma((X, G)),
            dma((Z,)), dma((Z,)),
        ],
        compiler_params=pltpu.CompilerParams(
            collective_id=0, has_side_effects=True, vmem_limit_bytes=58 * 1024 * 1024),
    )(tokens, idx, key_value_weight, adapter_down_weight.reshape(AR, F), adapter_up_weight.reshape(AR, N))


def solution(mesh):
    G, R, Z = (mesh.shape[a] for a in ("groups", "replica", "mp"))
    return jax.shard_map(
        functools.partial(shards, G, R, Z),
        mesh=mesh,
        in_specs=(
            P(("groups", "replica"), "mp"),
            P(("groups", "replica")),
            P(None, "mp"),
            P("replica", None, "mp"),
            P("replica", None, "mp"),
        ),
        out_specs=P(("groups", "replica"), "mp"),
        check_vma=False,
    )
```

time: 338 us -> 203 us (0.60)
  Pallas kernels: 0 us -> 197 us
  waiting for transfers between devices: 153 us -> 0 us
  blocking collectives: 128 us -> 0 us
  matrix products: 17.3 us -> 0 us
  between operations: 13.5 us -> 0.01 us
  local copies, waits for them, and re-layouts: 16 us -> 3.94 us
  other arithmetic: 9.21 us -> 0 us
    pallas_call x0 -> x1, Pallas kernels: none -> 197 us  [shards(): pl.pallas_call(functools.partial(kernel, G, R, Z, CH), out_shape=jax.Shap...]
    all_gather x1 -> x0, waiting for transfers between devices: 153 us -> none  [shards(): lax.all_gather(tokens, 'mp', axis=1, tiled=True)]
    all_to_all x2 -> x0, blocking collectives: 69.8 us -> none  [the longest x1 52.6 us: shards(): lax.all_to_all(outgoing, 'replica', split_axis=0, concat_axis=0, tiled=True)]
    psum x1 -> x0, blocking collectives: 58.6 us -> none  [shards(): reduced_input = lax.psum(partial_rank, 'mp').astype(jnp.bfloat16)]
    dot_general x3 -> x0, matrix products: 17.3 us -> none  [the longest x1 15.7 us: shards(): jnp.dot(lax.all_gather(tokens, 'mp', axis=1, tiled=True), key_value_weigh...]
    scatter x1 -> x0, local copies, waits for them, and re-layouts: 10.4 us -> none  [shards(): jnp.zeros((adapters_all * MOST, feat_width), jnp.bfloat16).at[slot_index]]
    another operation x3 -> x0, other arithmetic: 9.15 us -> none
    gather x1 -> x0, local copies, waits for them, and re-layouts: 5.07 us -> none  [shards(): delta_rows = returned[slot_index]]
  transfers between devices with their start and end apart: 1 -> 0, of which waited for: 1 -> 0; matrix products, arithmetic and copies ran while one was open for 8% -> 0% of each run, Pallas kernels for 0% -> 0%
where the time goes in v1:
time: 203 us; the launch traced here: 201 us
  Pallas kernels  197 us (97%)
  local copies, waits for them, and re-layouts  3.94 us (2%)
    pallas_call x1, Pallas kernels, shards(): pl.pallas_call(functools.partial(kernel, G, R, Z, CH), out_shape=jax.Shap...  197 us

profile of v1, /device:TPU:0, one launch (start us, length us, event | category | flops | bytes accessed | tf_op | source)
XLA Modules:
  0.0 201.2 jit_solution(479537778800080258)
XLA Ops:
  0.0 1.7 broadcast_in_dim.2.idx_ref
  1.7 197.3 %shard_map.55 = bf16[1024,512]{1,0:T(8,128)(2,1)} custom-call(bf16[1024,2048]{1,0:T(8,128)(2,1)} %tok_hbm.1, s32[1024,128]{1,0:T(8,128)} %broadcast_in_dim.2.idx_ref, bf16[8192,512]{1,0:T(8,128)(2,1)} %w_hbm.1, bf16[512,2048]{1,0:T(8,128)(2,1)} %bitcast.2, bf16[512,512]{1,0:T(8,128)(2,1)} %bitcast.3), custom_call_target="tpu_custom_call" | custom-call | tf_op jit(solution)/shard_map/pallas_call | solution.py:351
  198.9 2.3 %copy.7 = bf16[1024,512]{1,0:T(8,128)(2,1)} copy(bf16[1024,512]{1,0:T(8,128)(2,1)} %shard_map.55) | data formatting | bytes 2097152

commit v2 on v1

--- a/solution.py
+++ b/solution.py
@@ -16,7 +16,7 @@
     G, R, Z, CH,
     tok_hbm, idx_ref, w_hbm, down_hbm, up_hbm, out_ref,
     tok, wbuf, dbuf, from_left, from_right, sendbuf, low, lowin, base,
-    loc_sem, wz_s, wz_r, wp_s, wp_r, ws_s, ws_r,
+    loc_sem, wz_s, wz_r, wp_s, wp_r, wc_s, wc_r, ws_s, ws_r,
     rl_s, rl_r, rr_s, rr_r,
     d0_s, d0_r, d1_s, d1_r, d2_s, d2_r, d3_s, d3_r,
     lo_s, lo_r,
@@ -40,8 +40,8 @@
     sib = (g, x * 2 + 1 - c, z)
 
     def chip(k):
-        qq = lax.rem(q + k, C)
-        return qq, (qq // X, (qq % X) * 2 + c, z)
+        gg, xx = lax.rem(g + k // X, G), lax.rem(x + k % X, X)
+        return gg * X + xx, (gg, xx * 2 + c, z)
 
     barrier = pltpu.get_barrier_semaphore()
     for k in range(1, Z):
@@ -78,15 +78,37 @@
         ref = wbuf.at[b, wrows(g, r), :]
         return remote(ref, ref, wz_s.at[b], wz_r.at[b], (g, r, b))
 
-    def wp(b, k):
-        qq, dev = chip(k)
+    def wp(b, n):
         ref = wbuf.at[b, wrows(g, r), :]
-        return remote(ref, ref, wp_s.at[b, k], wp_r.at[b, q], dev)
-
-    def wp_in(b, k):
-        qq, dev = chip(k)
+        return remote(ref, ref, wp_s.at[b, n], wp_r.at[b, q], line(n)[1])
+
+    def line(n):
+        if n < X - 1:
+            gg, xx = g, lax.rem(x + n + 1, X)
+        else:
+            gg, xx = lax.rem(g + n - X + 2, G), x
+        return gg * X + xx, (gg, xx * 2 + c, z)
+
+    def wp_in(b, n):
+        qq, dev = line(n)
         ref = wbuf.at[b, wrows(qq // X, (qq % X) * 2 + c), :]
-        return remote(ref, ref, wp_s.at[b, k], wp_r.at[b, qq], dev)
+        return remote(ref, ref, wp_s.at[b, n], wp_r.at[b, qq], dev)
+
+    def half(gg, xx, h):
+        return pl.ds(pl.multiple_of((gg * R + xx * 2 + c) * FP + h * (FP // 2), FP // 2), FP // 2)
+
+    def wc(b, i, j, h):
+        gg, xx = lax.rem(g + j, G), lax.rem(x + i, X)
+        if h == 0:
+            ref, src, dev = wbuf.at[b, half(g, xx, 0), :], g * X + xx, (gg, r, z)
+        else:
+            ref, src, dev = wbuf.at[b, half(gg, x, 1), :], gg * X + x, (g, xx * 2 + c, z)
+        return remote(ref, ref, wc_s.at[b, (i * G + j) * 2 + h], wc_r.at[b, src * 2 + h], dev)
+
+    def wc_in(b, i, j, h):
+        gg, xx = lax.rem(g + j, G), lax.rem(x + i, X)
+        ref = wbuf.at[b, half(gg, xx, h), :]
+        return remote(ref, ref, wc_s.at[b, (i * G + j) * 2 + h], wc_r.at[b, (gg * X + xx) * 2 + h], (gg, r, z))
 
     def ws(b, k):
         qq, dev = chip(k)
@@ -98,16 +120,47 @@
         ref = wbuf.at[b, wrows(qq // X, (qq % X) * 2 + 1 - c), :]
         return remote(ref, ref, ws_s.at[b, qq], ws_r.at[b, qq], sib)
 
-    def gather_w(b):
+    LINES = X - 1 + G - 1
+
+    def gather_a(b):
         wz_in(b).wait_recv()
-        for k in range(1, C):
-            wp(b, k).start()
+        for n in range(LINES):
+            wp(b, n).start()
         ws(b, 0).start()
-        for k in range(1, C):
-            wp_in(b, k).wait_recv()
+
+    def gather_b(b):
+        for n in range(LINES):
+            wp_in(b, n).wait_recv()
+            if n < X - 1:
+                for j in range(1, G):
+                    wc(b, n + 1, j, 0).start()
+            else:
+                for i in range(1, X):
+                    wc(b, i, n - X + 2, 1).start()
+        for k in range(1, X):
             ws(b, k).start()
+        for j in range(1, G):
+            ws(b, X * j).start()
+
+    def gather_corner(b):
+        for i in range(1, X):
+            for j in range(1, G):
+                wc_in(b, i, j, 0).wait_recv()
+                wc_in(b, i, j, 1).wait_recv()
+                ws(b, X * j + i).start()
+
+    def gather_c(b):
         for k in range(C):
             ws_in(b, k).wait_recv()
+
+    def blocks(s, do_right, do_left):
+        @pl.when(Z - 1 - s > z)
+        def _():
+            do_right(Z - 1 - s)
+
+        @pl.when(s < z)
+        def _():
+            do_left(s)
 
     for s in range(Z - 1):
         @pl.when(Z - 1 - s > z)
@@ -158,6 +211,11 @@
         return remote(ref, ref, d3_s.at[xk(k), h], d3_r.at[xk(k), h], sib)
 
     lane_half = lax.broadcasted_iota(jnp.int32, (CH, 128), 1) // 64
+    BIG = min(512, T)
+    lane_big = lax.broadcasted_iota(jnp.int32, (BIG, 128), 1) // 64
+
+    def big(m):
+        return pl.ds(pl.multiple_of(m * BIG, BIG), BIG)
 
     def rows(m):
         return pl.ds(pl.multiple_of(m * CH, CH), CH)
@@ -167,22 +225,29 @@
     def shrink(rr):
         src = pl.ds(pl.multiple_of(rr * AR, AR), AR)
 
-        @pl.loop(0, M)
+        @pl.loop(0, T // BIG)
         def _(m):
             y = lax.dot_general(
-                tok[rows(m), :], dbuf[src, pl.ds(0, F)], (((1,), (1,)), ((), ())),
+                tok[big(m), :], dbuf[src, pl.ds(0, F)], (((1,), (1,)), ((), ())),
                 preferred_element_type=F32)
-            mine = idx_ref[rows(m), :] - rr * (AR // 64) - lane_half
-            part = low[rows(m), :]
+            mine = idx_ref[big(m), :] - rr * (AR // 64) - lane_big
+            part = low[big(m), :]
             for t in range(AR // 128):
                 part += jnp.where(mine == 2 * t, y[:, t * 128:(t + 1) * 128], 0.0)
-            low[rows(m), :] = part
+            low[big(m), :] = part
 
     cp_tok.wait()
     cp_d.wait()
     cp_u.wait()
+    for k in range(1, X):
+        d1(k).start()
     d0().start()
     shrink(r)
+    cp_w.wait()
+
+    @pl.loop(0, T // BIG)
+    def _(m):
+        base[big(m), :] = jnp.dot(tok[big(m), :], wbuf[z], preferred_element_type=F32)
 
     def to_right(b, m):
         return remote(sendbuf.at[b, rows(m), :], from_left.at[b, rows(m), :],
@@ -192,44 +257,66 @@
         return remote(sendbuf.at[b, rows(m), :], from_right.at[b, rows(m), :],
                       rr_s.at[b, m], rr_r.at[b, m], (g, r, lax.rem(z + Z - 1, Z)))
 
-    def chain(b, landed, make, first):
+    def chain_first(b, make):
+        @pl.loop(0, M)
+        def _(m):
+            sendbuf[b, rows(m), :] = jnp.dot(
+                tok[rows(m), :], wbuf[b], preferred_element_type=F32).astype(BF16)
+            make(b, m).start()
+
+    def chain(b, landed, make):
         @pl.loop(0, M)
         def _(m):
             y = jnp.dot(tok[rows(m), :], wbuf[b], preferred_element_type=F32)
-
-            @pl.when(first)
-            def _():
-                sendbuf[b, rows(m), :] = y.astype(BF16)
-
-            @pl.when(jnp.logical_not(first))
-            def _():
-                make(b, m).wait_recv()
-                sendbuf[b, rows(m), :] = (y + landed[b, rows(m), :].astype(F32)).astype(BF16)
-
+            make(b, m).wait_recv()
+            sendbuf[b, rows(m), :] = (y + landed[b, rows(m), :].astype(F32)).astype(BF16)
             make(b, m).start()
 
+    def middle(k):
+        right = Z - 1 + z - k
+
+        @pl.when((z > 0) & (right > z) & (right < Z))
+        def _():
+            chain(right, from_left, to_right)
+
+        left = k - (Z - 1 - z)
+
+        @pl.when((z < Z - 1) & (left >= 0) & (left < z))
+        def _():
+            chain(left, from_right, to_left)
+
+    def finish_right(b):
+        gather_corner(b)
+        gather_c(b)
+
+        @pl.when(z == 0)
+        def _():
+            chain_first(b, to_right)
+
+    def finish_left(b):
+        gather_corner(b)
+        gather_c(b)
+
+        @pl.when(z == Z - 1)
+        def _():
+            chain_first(b, to_left)
+
+    blocks(0, gather_a, gather_a)
     for s in range(Z - 1):
-        @pl.when(Z - 1 - s > z)
-        def _(b=Z - 1 - s):
-            gather_w(b)
-            chain(b, from_left, to_right, z == 0)
-
-        @pl.when(s < z)
-        def _(b=s):
-            gather_w(b)
-            chain(b, from_right, to_left, z == Z - 1)
-
-        if s == 0:
-            for k in range(1, X):
-                d1(k).start()
-
+        blocks(s, gather_b, gather_b)
+        if s + 1 < Z - 1:
+            blocks(s + 1, gather_a, gather_a)
+        blocks(s, finish_right, finish_left)
+
+    d0_in().wait_recv()
+    shrink(x * 2 + 1 - c)
     for k in range(1, X):
         d1_in(k).wait_recv()
         for j in range(1, G):
             d2(k, j).start()
         d3(k, g).start()
-    d0_in().wait_recv()
-    shrink(x * 2 + 1 - c)
+    if Z > 2:
+        middle(1)
     for k in range(1, X):
         for j in range(1, G):
             d2_in(k, j).wait_recv()
@@ -257,11 +344,9 @@
     for k in range(1, Z):
         lo(k).start()
 
-    cp_w.wait()
-
-    @pl.loop(0, M)
-    def _(m):
-        base[rows(m), :] = jnp.dot(tok[rows(m), :], wbuf[z], preferred_element_type=F32)
+    if Z > 2:
+        for k in range(2, Z - 1):
+            middle(k)
 
     total = packed
     for k in range(1, Z):
@@ -272,10 +357,10 @@
     low[pl.ds(0, H), :] = jnp.where(left_lanes, total, other)
     low[pl.ds(H, H), :] = jnp.where(left_lanes, other, total)
 
-    @pl.loop(0, M)
+    @pl.loop(0, T // BIG)
     def _(m):
-        ss = low[rows(m), :]
-        who = idx_ref[rows(m), :] - lane_half
+        ss = low[big(m), :]
+        who = idx_ref[big(m), :] - lane_big
 
         def add(rr, acc):
             lhs = jnp.concatenate(
@@ -285,8 +370,8 @@
                 lhs, dbuf[pl.ds(pl.multiple_of(rr * AR, AR), AR), pl.ds(F, N)],
                 preferred_element_type=F32)
 
-        delta = lax.fori_loop(0, R, add, jnp.zeros((CH, N), F32))
-        base[rows(m), :] = base[rows(m), :] + delta.astype(BF16).astype(F32)
+        delta = lax.fori_loop(0, R, add, jnp.zeros((BIG, N), F32))
+        base[big(m), :] = base[big(m), :] + delta.astype(BF16).astype(F32)
 
     @pl.when(z > 0)
     def _():
@@ -308,8 +393,12 @@
         @pl.when(b != z)
         def _(b=b):
             wz(b).wait_send()
-            for k in range(1, C):
-                wp(b, k).wait_send()
+            for n in range(LINES):
+                wp(b, n).wait_send()
+            for i in range(1, X):
+                for j in range(1, G):
+                    wc(b, i, j, 0).wait_send()
+                    wc(b, i, j, 1).wait_send()
             for k in range(C):
                 ws(b, k).wait_send()
 
@@ -363,7 +452,7 @@
             pltpu.VMEM((T, 128), F32),
             pltpu.VMEM((Z, T // 2, 128), BF16),
             pltpu.VMEM((T, N), F32),
-            dma((4,)), dma((Z,)), dma((Z,)), dma((Z, C)), dma((Z, C)), dma((Z, C)), dma((Z, C)),
+            dma((4,)), dma((Z,)), dma((Z,)), dma((Z, C)), dma((Z, C)), dma((Z, 2 * C)), dma((Z, 2 * C)), dma((Z, C)), dma((Z, C)),
             dma((Z, M)), dma((Z, M)), dma((Z, M)), dma((Z, M)),
             dma, dma, dma((X,)), dma((X,)), dma((X, G)), dma((X, G)), dma((X, G)), dma((X, G)),
             dma((Z,)), dma((Z,)),

time: 203 us -> 143 us (0.70)
  Pallas kernels: 197 us -> 138 us
    pallas_call x1, Pallas kernels: 197 us -> 138 us  [shards(): pl.pallas_call(functools.partial(kernel, G, R, Z, CH), out_shape=jax.Shap...]
where the time goes in v2:
time: 143 us; the launch traced here: 141 us
  Pallas kernels  138 us (97%)
  local copies, waits for them, and re-layouts  3.94 us (3%)
    pallas_call x1, Pallas kernels, shards(): pl.pallas_call(functools.partial(kernel, G, R, Z, CH), out_shape=jax.Shap...  138 us

profile of v2, /device:TPU:0, one launch (start us, length us, event | category | flops | bytes accessed | tf_op | source)
XLA Modules:
  0.0 141.5 jit_solution(15171807963553217641)
XLA Ops:
  0.0 1.7 %broadcast_in_dim.2.idx_ref = s32[1024,128]{1,0:T(8,128)} broadcast(s32[1024]{0:T(1024)} %param.6), dimensions={0} | broadcast | bytes 528384 | tf_op jit(solution)/shard_map/broadcast_in_dim | solution.py:436
  1.7 137.5 %shard_map.55 = bf16[1024,512]{1,0:T(8,128)(2,1)} custom-call(bf16[1024,2048]{1,0:T(8,128)(2,1)} %tok_hbm.1, s32[1024,128]{1,0:T(8,128)} %broadcast_in_dim.2.idx_ref, bf16[8192,512]{1,0:T(8,128)(2,1)} %w_hbm.1, bf16[512,2048]{1,0:T(8,128)(2,1)} %bitcast.2, bf16[512,512]{1,0:T(8,128)(2,1)} %bitcast.3), custom_call_target="tpu_custom_call" | custom-call | tf_op jit(solution)/shard_map/pallas_call | solution.py:440
  139.2 2.3 %copy.7 = bf16[1024,512]{1,0:T(8,128)(2,1)} copy(bf16[1024,512]{1,0:T(8,128)(2,1)} %shard_map.55) | data formatting | bytes 2097152

commit v3 on v2

--- a/solution.py
+++ b/solution.py
@@ -307,14 +307,15 @@
         if s + 1 < Z - 1:
             blocks(s + 1, gather_a, gather_a)
         blocks(s, finish_right, finish_left)
+        if s == 0:
+            for k in range(1, X):
+                d1_in(k).wait_recv()
+                for j in range(1, G):
+                    d2(k, j).start()
+                d3(k, g).start()
 
     d0_in().wait_recv()
     shrink(x * 2 + 1 - c)
-    for k in range(1, X):
-        d1_in(k).wait_recv()
-        for j in range(1, G):
-            d2(k, j).start()
-        d3(k, g).start()
     if Z > 2:
         middle(1)
     for k in range(1, X):

time: 143 us -> 157 us (1.098)
  the two profiles are of different devices: /device:TPU:0 before, /device:TPU:9 now
where the time goes in v3:
time: 157 us
  Pallas kernels  153 us (97%)
  local copies, waits for them, and re-layouts  3.94 us (3%)
    pallas_call x1, Pallas kernels, shards(): pl.pallas_call(functools.partial(kernel, G, R, Z, CH), out_shape=jax.Shap...  153 us

profile of v3, /device:TPU:9, one launch (start us, length us, event | category | flops | bytes accessed | tf_op | source)
XLA Modules:
  0.0 157.1 jit_solution(12914844984412396186)
XLA Ops:
  0.0 1.7 %broadcast_in_dim.2.idx_ref = s32[1024,128]{1,0:T(8,128)} broadcast(s32[1024]{0:T(1024)} %param.6), dimensions={0} | broadcast | bytes 528384 | tf_op jit(solution)/shard_map/broadcast_in_dim | solution.py:437
  1.7 153.1 %shard_map.55 = bf16[1024,512]{1,0:T(8,128)(2,1)} custom-call(bf16[1024,2048]{1,0:T(8,128)(2,1)} %tok_hbm.1, s32[1024,128]{1,0:T(8,128)} %broadcast_in_dim.2.idx_ref, bf16[8192,512]{1,0:T(8,128)(2,1)} %w_hbm.1, bf16[512,2048]{1,0:T(8,128)(2,1)} %bitcast.2, bf16[512,512]{1,0:T(8,128)(2,1)} %bitcast.3), custom_call_target="tpu_custom_call" | custom-call | tf_op jit(solution)/shard_map/pallas_call | solution.py:441
  154.8 2.3 %copy.7 = bf16[1024,512]{1,0:T(8,128)(2,1)} copy(bf16[1024,512]{1,0:T(8,128)(2,1)} %shard_map.55) | data formatting | bytes 2097152
